TPU v7x, 32 devices: a whole 2x2x4 slice. The times are simulated.
32 devices in a mesh: row: 8 (over z, y), col: 4 (over x, core).
Axes of the slice: x: 2, y: 2, z: 4, core: 2. Of those that a mesh axis runs over, the one named last changes fastest.
Arguments:
- tile_values: bfloat16 [8, 4, 4, 256, 256], P('row', 'col'), may hold values from -0.125 to 0.125
- tile_row: int32 [8, 4, 4], P('row', 'col'), may hold values from 0 to 3
- tile_col: int32 [8, 4, 4], P('row', 'col'), may hold values from 0 to 7
- basis_init: bfloat16 [32, 8192], P(None, ('col', 'row')), may hold values from -6 to 6
Outputs:
- ritz_basis: float32 [32, 8192], P(None, ('col', 'row'))
- residual: float32 [32, 8192], P(None, ('col', 'row'))
- projected: float32 [32, 32], replicated
Inputs may be any that keep to these rules, and one draw needn't show every extreme that they name: `tile_row`: coordinates may repeat within a pair of blocks; repeated tiles add. `tile_col`: coordinates may repeat within a pair of blocks; repeated tiles add.
All inputs are finite; a program needn't handle non-finite values.
Results may differ from a plain program's by a relative error of at most 0.013.
Values may be sent and summed in bfloat16 or wider, within the bound.
A program may use at most 64 MiB of HBM per device.

v0:
```python
import jax
import jax.numpy as jnp
from jax import lax
from jax.sharding import PartitionSpec as P


def exact_dot(left, right):
    return jnp.dot(left, right, precision=lax.Precision.HIGHEST)


def bucket(contrib, index, slots):
    tile_size = contrib.shape[-1]
    onehot_table = (index[:, None] == jnp.arange(slots, dtype=jnp.int32)[None, :]).astype(
        jnp.float32
    )
    summed = jnp.einsum("ktb,tn->knb", contrib, onehot_table, precision=lax.Precision.HIGHEST)
    return summed.reshape(contrib.shape[0], slots * tile_size)


def apply_hamiltonian(tile_block, tile_rows, tile_cols, vectors_bf):
    vector_count = vectors_bf.shape[0]
    local_rows = vectors_bf.shape[1]
    tile_size = tile_block.shape[-1]
    row_tiles = lax.axis_size("col") * local_rows // tile_size
    col_tiles = lax.axis_size("row") * local_rows // tile_size
    column_block = lax.all_gather(vectors_bf, "row", axis=1, tiled=True)
    row_block = lax.all_gather(vectors_bf, "col", axis=1, tiled=True)
    picked = column_block.reshape(vector_count, col_tiles, tile_size)[:, tile_cols]
    direct = jnp.einsum("ktj,tij->kti", picked, tile_block, preferred_element_type=jnp.float32)
    mirror_pick = row_block.reshape(vector_count, row_tiles, tile_size)[:, tile_rows]
    mirror = jnp.einsum("kti,tij->ktj", mirror_pick, tile_block, preferred_element_type=jnp.float32)
    direct_part = bucket(direct, tile_rows, row_tiles)
    mirror_part = bucket(mirror, tile_cols, col_tiles)
    own_direct = lax.psum_scatter(
        direct_part.astype(jnp.bfloat16), "col", scatter_dimension=1, tiled=True
    ).astype(jnp.float32)
    mirror_total = lax.psum(mirror_part.astype(jnp.bfloat16), "row").astype(jnp.float32)
    own_mirror = lax.dynamic_slice_in_dim(
        mirror_total, lax.axis_index("row") * local_rows, local_rows, 1
    )
    return own_direct + own_mirror


def shards(tile_values, tile_row, tile_col, basis_init):
    tile_block = tile_values[0, 0]
    tile_rows = tile_row[0, 0]
    tile_cols = tile_col[0, 0]
    total_rows = basis_init.shape[1] * lax.axis_size("row") * lax.axis_size("col")
    current = basis_init
    ritz_basis = basis_init.astype(jnp.float32)
    product_block = apply_hamiltonian(tile_block, tile_rows, tile_cols, current)
    gram_matrix = lax.psum(exact_dot(product_block, product_block.T), ("row", "col")) / total_rows
    factor = jnp.linalg.cholesky(gram_matrix)
    ritz_basis = lax.linalg.triangular_solve(factor, product_block, left_side=True, lower=True)
    current = ritz_basis.astype(jnp.bfloat16)
    product_block = apply_hamiltonian(tile_block, tile_rows, tile_cols, current)
    projected = lax.psum(exact_dot(ritz_basis, product_block.T), ("row", "col")) / total_rows
    residual = product_block - exact_dot(projected.T, ritz_basis)
    return (ritz_basis, residual, projected)


def solution(mesh):
    return jax.shard_map(
        shards,
        mesh=mesh,
        in_specs=(
            P("row", "col", None, None, None),
            P("row", "col", None),
            P("row", "col", None),
            P(None, ("col", "row")),
        ),
        out_specs=(P(None, ("col", "row")), P(None, ("col", "row")), P()),
        check_vma=False,
    )
```

profile of v0, /device:TPU:0, one launch (start us, length us, event | category | flops | bytes accessed | tf_op | source)
XLA Modules:
  0.0 331.4 jit_solution(4178294766963802984)
XLA Ops:
  8.1 32.7 %all_gather.12 = bf16[32,2048]{1,0:T(8,128)(2,1)S(1)} all-gather(bf16[32,256]{1,0:T(8,128)(2,1)} %param.7), channel_id=1, replica_groups=mesh['row'=8,'col'=4] {'row'}, dimensions={1}, use_global_device_ids=true | all-gather | bytes 147456 | tf_op jit(solution)/shard_map/all_gather | solution.py:26
  40.7 0.6 copy-done.6
  41.4 0.6 gather_fusion
  42.2 0.7 copy-done.5
  43.2 0.6 copy.35
  43.9 0.6 copy-done.2
  44.5 5.2 %all_gather.13 = bf16[32,1024]{1,0:T(8,128)(2,1)S(1)} all-gather(bf16[32,256]{1,0:T(8,128)(2,1)S(1)} %copy-done.2), channel_id=1, replica_groups=mesh['row'=8,'col'=4] {'col'}, dimensions={1}, use_global_device_ids=true | all-gather | bytes 81920 | tf_op jit(solution)/shard_map/all_gather | solution.py:27
  49.8 0.6 gather_fusion.1
  50.5 0.4 convolution_convert_fusion.1
  51.0 0.7 copy.36
  51.7 12.7 %reduce-scatter.3.cloned.1.call-done = bf16[32,256]{1,0:T(8,128)(2,1)} async-done(((bf16[32,1024]{1,0:T(8,128)(2,1)}), bf16[32,256]{1,0:T(8,128)(2,1)}) %reduce-scatter.3.cloned.1.call-update) | async-done | bytes 16400 | tf_op jit(solution)/shard_map/reduce_scatter | solution.py:34
  64.4 57.6 %all-reduce.3.cloned.1.call-done = bf16[32,2048]{1,0:T(8,128)(2,1)} async-done(((bf16[32,2048]{1,0:T(8,128)(2,1)}), bf16[32,2048]{1,0:T(8,128)(2,1)}) %all-reduce.3.cloned.1.call-update) | async-done | bytes 131088 | tf_op jit(solution)/shard_map/psum | solution.py:37
  121.9 1.0 fusion.13
  122.9 39.8 %psum.29 = f32[32,32]{0,1:T(8,128)S(1)} all-reduce(f32[32,32]{0,1:T(8,128)S(1)} %fusion.13), channel_id=1, replica_groups=mesh['row'=8,'col'=4] {'row','col'}, use_global_device_ids=true, to_apply=%region_2.0 | all-reduce | flops 1024 | bytes 8192 | tf_op jit(solution)/shard_map/psum | solution.py:52
  162.8 2.9 cholesky.16
  165.7 0.6 compare_reduce_fusion
  166.4 0.7 fusion.15
  167.0 2.4 custom-call.6
  169.5 1.0 fusion.36
  170.5 30.5 %all_gather.14 = bf16[32,2048]{1,0:T(8,128)(2,1)S(1)} all-gather(bf16[32,256]{1,0:T(8,128)(2,1)S(1)} %get-tuple-element.12), channel_id=1, replica_groups=mesh['row'=8,'col'=4] {'row'}, dimensions={1}, use_global_device_ids=true | all-gather | bytes 147456 | tf_op jit(solution)/shard_map/all_gather | solution.py:26
  201.0 5.6 %all_gather.15 = bf16[32,1024]{1,0:T(8,128)(2,1)S(1)} all-gather(bf16[32,256]{1,0:T(8,128)(2,1)S(1)} %get-tuple-element.12), channel_id=1, replica_groups=mesh['row'=8,'col'=4] {'col'}, dimensions={1}, use_global_device_ids=true | all-gather | bytes 81920 | tf_op jit(solution)/shard_map/all_gather | solution.py:27
  206.6 0.6 gather_fusion.2
  207.7 0.6 copy.37
  208.4 0.6 gather_fusion.3
  209.2 0.4 convolution_convert_fusion
  209.6 0.7 copy.38
  210.3 16.9 %reduce-scatter.5.cloned.1.call-done = bf16[32,256]{1,0:T(8,128)(2,1)} async-done(((bf16[32,1024]{1,0:T(8,128)(2,1)}), bf16[32,256]{1,0:T(8,128)(2,1)}) %reduce-scatter.5.cloned.1.call-update) | async-done | bytes 16400 | tf_op jit(solution)/shard_map/reduce_scatter | solution.py:34
  227.3 53.8 %all-reduce.5.cloned.1.call-done = bf16[32,2048]{1,0:T(8,128)(2,1)} async-done(((bf16[32,2048]{1,0:T(8,128)(2,1)}), bf16[32,2048]{1,0:T(8,128)(2,1)}) %all-reduce.5.cloned.1.call-update) | async-done | bytes 131088 | tf_op jit(solution)/shard_map/psum | solution.py:37
  281.1 0.9 fusion.14
  282.0 39.8 %psum.31 = f32[32,32]{0,1:T(8,128)S(1)} all-reduce(f32[32,32]{0,1:T(8,128)S(1)} %fusion.14), channel_id=1, replica_groups=mesh['row'=8,'col'=4] {'row','col'}, use_global_device_ids=true, to_apply=%region_7.8 | all-reduce | flops 1024 | bytes 8192 | tf_op jit(solution)/shard_map/psum | solution.py:57
  321.8 0.7 copy.28
  322.5 1.5 convolution_subtract_fusion
  (38 shorter events, 2.0 us)
Async XLA Ops:
  8.0 33.9 %copy-start = (bf16[1,1,4,256,256]{4,3,2,1,0:T(8,128)(2,1)S(1)}, bf16[1,1,4,256,256]{4,3,2,1,0:T(8,128)(2,1)}, u32[]{:S(2)}) copy-start(bf16[1,1,4,256,256]{4,3,2,1,0:T(8,128)(2,1)} %param.4) | copy-start | bytes 1572868
  8.0 56.4 %reduce-scatter.3.cloned.1.call-start = ((), (), s32[]{:S(2)}) async-start(), calls=%async_computation.2 | async-start | bytes 81920 | tf_op jit(solution)/shard_map/reduce_scatter | solution.py:34
  40.7 0.7 copy-start.6
  42.2 0.7 copy-start.5
  43.8 0.7 copy-start.2
  43.8 78.1 %all-reduce.3.cloned.1.call-start = ((), (), s32[]{:S(2)}) async-start(), calls=%async_computation.3 | async-start | bytes 262144 | tf_op jit(solution)/shard_map/psum | solution.py:37
  51.7 175.6 %reduce-scatter.5.cloned.1.call-start = ((), (), s32[]{:S(2)}) async-start(), calls=%async_computation.4 | async-start | bytes 81920 | tf_op jit(solution)/shard_map/reduce_scatter | solution.py:34
  166.4 3.1 copy-start.4
  170.4 152.0 %copy-start.1 = (f32[32,256]{1,0:T(8,128)}, f32[32,256]{1,0:T(8,128)S(1)}, u32[]{:S(2)}) copy-start(f32[32,256]{1,0:T(8,128)S(1)} %get-tuple-element.13) | copy-start | bytes 98308
  208.4 72.7 %all-reduce.5.cloned.1.call-start = ((), (), s32[]{:S(2)}) async-start(), calls=%async_computation.5 | async-start | bytes 262144 | tf_op jit(solution)/shard_map/psum | solution.py:37
  321.8 0.7 copy-start.3
Sparse Core Ops, SparseCore 0:
  44.0 20.3 reduce-scatter.2
  208.5 18.7 reduce-scatter.4
Sparse Core Ops, SparseCore 1:
  51.8 70.1 all-reduce.2
  212.6 68.5 all-reduce.4
where the time goes:
time: 332 us; the launch traced here: 331 us
  blocking collectives  154 us (46%)
  waiting for transfers between devices  141 us (42%)
  between operations  15.6 us (5%)
  local copies, waits for them, and re-layouts  7.62 us (2%)
  other arithmetic  6.73 us (2%)
  matrix products  6.68 us (2%)
    psum x2, waiting for transfers between devices, apply_hamiltonian(): lax.psum(mirror_part.astype(jnp.bfloat16), 'row').astype(jnp.float32)  111 us
    all_gather x2, blocking collectives, apply_hamiltonian(): column_block = lax.all_gather(vectors_bf, 'row', axis=1, tiled=True)  63.2 us
    psum x1, blocking collectives, shards(): lax.psum(exact_dot(product_block, product_block.T), ('row', 'col'))  39.8 us
    psum x1, blocking collectives, shards(): lax.psum(exact_dot(ritz_basis, product_block.T), ('row', 'col'))  39.8 us
    reduce_scatter x2, waiting for transfers between devices, apply_hamiltonian(): lax.psum_scatter(direct_part.astype(jnp.bfloat16), 'col', scatter_dimensi...  29.6 us
    all_gather x2, blocking collectives, apply_hamiltonian(): row_block = lax.all_gather(vectors_bf, 'col', axis=1, tiled=True)  10.8 us
  transfers between devices with their start and end apart: 4, of which 4 were waited for; matrix products, arithmetic and copies ran while one was open for 1% of the time, Pallas kernels for 0%

commit v1 on v0

v1 whole, which is shorter than its diff:
```python
import functools

import jax
import jax.numpy as jnp
from jax import lax
from jax.experimental import pallas as pl
from jax.experimental.pallas import tpu as pltpu
from jax.sharding import PartitionSpec as P

MESH = pl.DeviceIdType.MESH
F32 = jnp.float32
BF16 = jnp.bfloat16
NT = (((1,), (1,)), ((), ()))


def exact_dot(left, right):
    return jnp.dot(left, right, precision=lax.Precision.HIGHEST, preferred_element_type=F32)


def exact_dot_nt(left, right):
    return lax.dot_general(
        left, right, NT, precision=lax.Precision.HIGHEST, preferred_element_type=F32
    )


def offsets(size):
    return sorted(range(1, size), key=lambda d: -min(d, size - d))


def pack(square):
    k = square.shape[0]
    per = 128 // k
    rows = k // per
    return jnp.concatenate([square[i * rows : (i + 1) * rows] for i in range(per)], axis=1)


def unpack(packed, k):
    per = 128 // k
    return jnp.concatenate([packed[:, i * k : (i + 1) * k] for i in range(per)], axis=0)


def inverse_factor(gram):
    k = gram.shape[0]
    row_id = lax.broadcasted_iota(jnp.int32, (k, 2 * k), 0)
    eye = (
        lax.broadcasted_iota(jnp.int32, (k, k), 0) == lax.broadcasted_iota(jnp.int32, (k, k), 1)
    ).astype(F32)
    work = jnp.concatenate([gram, eye], axis=1)
    out = jnp.zeros((k, 2 * k), F32)
    for i in range(k):
        scale = lax.rsqrt(work[i : i + 1, i : i + 1])
        row = work[i : i + 1, :] * scale
        column = work[:, i : i + 1] * scale
        out = jnp.where(row_id == i, row, out)
        if i < k - 1:
            work = work - column * row
    return out[:, k:]


def kernel(
    n_row, n_col, total_rows,
    tiles_ref, trow_ref, tcol_ref, x_ref,
    ritz_ref, res_ref, proj_ref,
    col_x, row_x, y_bf, dir_out, mir_out, dir_in, mir_in, small_row, small_col,
    send_sem, recv_sem,
):
    my_row = lax.axis_index("row")
    my_col = lax.axis_index("col")
    tile_count = tiles_ref.shape[0]
    k = x_ref.shape[0]

    def row_peer(d):
        return (lax.rem(my_row + d, n_row), my_col)

    def col_peer(d):
        return (my_row, lax.rem(my_col + d, n_col))

    barrier = pltpu.get_barrier_semaphore()
    for d in range(1, n_row):
        pl.semaphore_signal(barrier, inc=1, device_id=row_peer(d), device_id_type=MESH)
    for d in range(1, n_col):
        pl.semaphore_signal(barrier, inc=1, device_id=col_peer(d), device_id_type=MESH)

    col_x[0, my_row] = x_ref[...]
    row_x[0, my_col] = x_ref[...]
    pl.semaphore_wait(barrier, n_row + n_col - 2)

    def send(src, dst, channel, peer):
        pltpu.make_async_remote_copy(
            src_ref=src, dst_ref=dst, send_sem=send_sem.at[channel], recv_sem=recv_sem.at[channel],
            device_id=peer, device_id_type=MESH,
        ).start()

    def wait_in(ref, channel):
        pltpu.make_async_copy(ref, ref, recv_sem.at[channel]).wait()

    def wait_out(ref, channel):
        pltpu.make_async_copy(ref, ref, send_sem.at[channel]).wait()

    def gather_start(src, p):
        for d in offsets(n_row):
            send(src, col_x.at[p, my_row], 4 * p, row_peer(d))
        for d in offsets(n_col):
            send(src, row_x.at[p, my_col], 4 * p + 1, col_peer(d))

    def gather_wait(p):
        wait_in(col_x.at[p, pl.ds(0, n_row - 1)], 4 * p)
        wait_in(row_x.at[p, pl.ds(0, n_col - 1)], 4 * p + 1)

    def small_start(p, which):
        if which == 0:
            for d in offsets(n_row):
                send(small_row.at[p, my_row], small_row.at[p, my_row], 8 + 2 * p, row_peer(d))
        else:
            for d in offsets(n_col):
                send(small_col.at[p, my_col], small_col.at[p, my_col], 9 + 2 * p, col_peer(d))

    def small_sum(p, which):
        ref, size = ((small_row, n_row), (small_col, n_col))[which]
        wait_in(ref.at[p, pl.ds(0, size - 1)], 8 + 2 * p + which)
        value = ref[p, 0]
        for i in range(1, size):
            value = value + ref[p, i]
        return value

    def products(p):
        direct, mirror, row_picks = [], [], []
        for t in range(tile_count):
            picked = col_x[p, tcol_ref[t]]
            direct.append(
                lax.dot_general(picked, tiles_ref[t], NT, preferred_element_type=F32)
            )
            row_pick = row_x[p, trow_ref[t]]
            row_picks.append(row_pick)
            mirror.append(jnp.dot(row_pick, tiles_ref[t], preferred_element_type=F32))
        return direct, mirror, row_picks

    def bucket(parts, index_ref, slot):
        value = None
        for t in range(tile_count):
            term = jnp.where(index_ref[t] == slot, parts[t], 0.0)
            value = term if value is None else value + term
        return value.astype(BF16)

    def scatter_start(p, direct, mirror):
        for n in range(n_row):
            mir_out[p, n] = bucket(mirror, tcol_ref, n)
        for d in offsets(n_row):
            peer = row_peer(d)
            send(mir_out.at[p, peer[0]], mir_in.at[p, d - 1], 4 * p + 2, peer)
        for n in range(n_col):
            dir_out[p, n] = bucket(direct, trow_ref, n)
        for d in offsets(n_col):
            peer = col_peer(d)
            send(dir_out.at[p, peer[1]], dir_in.at[p, d - 1], 4 * p + 3, peer)

    def scatter_sum(p):
        value = dir_out[p, my_col].astype(F32) + mir_out[p, my_row].astype(F32)
        wait_in(dir_in.at[p], 4 * p + 3)
        for i in range(n_col - 1):
            value = value + dir_in[p, i].astype(F32)
        wait_in(mir_in.at[p], 4 * p + 2)
        for i in range(n_row - 1):
            value = value + mir_in[p, i].astype(F32)
        return value

    gather_start(x_ref, 0)
    gather_wait(0)
    direct, mirror, _ = products(0)
    scatter_start(0, direct, mirror)
    image = scatter_sum(0)

    y_bf[...] = image.astype(BF16)
    gather_start(y_bf, 1)
    col_x[1, my_row] = y_bf[...]
    row_x[1, my_col] = y_bf[...]
    small_row[0, my_row] = pack(exact_dot_nt(image, image))
    small_start(0, 0)
    gather_wait(1)
    direct, mirror, row_picks = products(1)
    cross = None
    for t in range(tile_count):
        high = direct[t].astype(BF16)
        low = (direct[t] - high.astype(F32)).astype(BF16)
        for part in (high, low):
            term = lax.dot_general(row_picks[t], part, NT, preferred_element_type=F32)
            cross = term if cross is None else cross + term
    small_row[1, my_row] = pack(cross)
    small_start(1, 0)
    small_col[0, my_col] = small_sum(0, 0)
    small_start(0, 1)
    scatter_start(1, direct, mirror)
    gram = unpack(small_sum(0, 1), k) / total_rows
    small_col[1, my_col] = small_sum(1, 0)
    small_start(1, 1)
    inverse = inverse_factor(gram)
    ritz = exact_dot(inverse, image)
    ritz_ref[...] = ritz
    half = unpack(small_sum(1, 1), k) / total_rows
    half = exact_dot_nt(exact_dot(inverse, half), inverse)
    projected = half + half.T
    proj_ref[...] = projected
    last = scatter_sum(1)
    res_ref[...] = exact_dot(inverse, last) - exact_dot(projected, ritz)

    for p in range(2):
        wait_out(col_x.at[p, pl.ds(0, n_row - 1)], 4 * p)
        wait_out(row_x.at[p, pl.ds(0, n_col - 1)], 4 * p + 1)
        wait_out(mir_in.at[p], 4 * p + 2)
        wait_out(dir_in.at[p], 4 * p + 3)
        wait_out(small_row.at[p, pl.ds(0, n_row - 1)], 8 + 2 * p)
        wait_out(small_col.at[p, pl.ds(0, n_col - 1)], 9 + 2 * p)


def shards(n_row, n_col, tile_values, tile_row, tile_col, basis_init):
    k, m = basis_init.shape
    tiles = tile_values[0, 0]
    total_rows = m * n_row * n_col
    packed = (k * k // 128, 128)
    vmem = pl.BlockSpec(memory_space=pltpu.VMEM)
    smem = pl.BlockSpec(memory_space=pltpu.SMEM)
    return pl.pallas_call(
        functools.partial(kernel, n_row, n_col, total_rows),
        out_shape=(
            jax.ShapeDtypeStruct((k, m), F32),
            jax.ShapeDtypeStruct((k, m), F32),
            jax.ShapeDtypeStruct((k, k), F32),
        ),
        in_specs=[vmem, smem, smem, vmem],
        out_specs=(vmem, vmem, vmem),
        scratch_shapes=[
            pltpu.VMEM((2, n_row, k, m), BF16),
            pltpu.VMEM((2, n_col, k, m), BF16),
            pltpu.VMEM((k, m), BF16),
            pltpu.VMEM((2, n_col, k, m), BF16),
            pltpu.VMEM((2, n_row, k, m), BF16),
            pltpu.VMEM((2, n_col - 1, k, m), BF16),
            pltpu.VMEM((2, n_row - 1, k, m), BF16),
            pltpu.VMEM((2, n_row) + packed, F32),
            pltpu.VMEM((2, n_col) + packed, F32),
            pltpu.SemaphoreType.DMA((12,)),
            pltpu.SemaphoreType.DMA((12,)),
        ],
        compiler_params=pltpu.CompilerParams(
            collective_id=0, has_side_effects=True, vmem_limit_bytes=32 * 1024 * 1024
        ),
    )(tiles, tile_row[0, 0], tile_col[0, 0], basis_init)


def solution(mesh):
    return jax.shard_map(
        functools.partial(shards, mesh.shape["row"], mesh.shape["col"]),
        mesh=mesh,
        in_specs=(
            P("row", "col", None, None, None),
            P("row", "col", None),
            P("row", "col", None),
            P(None, ("col", "row")),
        ),
        out_specs=(P(None, ("col", "row")), P(None, ("col", "row")), P()),
        check_vma=False,
    )
```

time: 332 us -> 38.5 us (0.12)
  blocking collectives: 154 us -> 0 us
  waiting for transfers between devices: 141 us -> 0 us
  Pallas kernels: 0 us -> 33.3 us
  between operations: 15.6 us -> 0.66 us
  other arithmetic: 6.73 us -> 0 us
  matrix products: 6.68 us -> 0 us
  local copies, waits for them, and re-layouts: 7.62 us -> 4.25 us
    psum x2 -> x0, waiting for transfers between devices: 111 us -> none  [apply_hamiltonian(): lax.psum(mirror_part.astype(jnp.bfloat16), 'row').astype(jnp.float32)]
    psum x2 -> x0, blocking collectives: 79.5 us -> none  [the longest x1 39.8 us: shards(): lax.psum(exact_dot(product_block, product_block.T), ('row', 'col'))]
    all_gather x4 -> x0, blocking collectives: 74 us -> none  [the longest x2 63.2 us: apply_hamiltonian(): column_block = lax.all_gather(vectors_bf, 'row', axis=1, tiled=True)]
    pallas_call x0 -> x1, Pallas kernels: none -> 33.3 us  [shards(): pl.pallas_call(functools.partial(kernel, n_row, n_col, total_rows), out_s...]
    reduce_scatter x2 -> x0, waiting for transfers between devices: 29.6 us -> none  [apply_hamiltonian(): lax.psum_scatter(direct_part.astype(jnp.bfloat16), 'col', scatter_dimensi...]
    another operation x5 -> x0, other arithmetic: 6.69 us -> none  [the longest x3 3.6 us: shards(): factor = jnp.linalg.cholesky(gram_matrix)]
    dot_general x11 -> x0, matrix products: 5.71 us -> none  [the longest x3 3.34 us: exact_dot(): return jnp.dot(left, right, precision=lax.Precision.HIGHEST)]
  transfers between devices with their start and end apart: 4 -> 0, of which waited for: 4 -> 0; matrix products, arithmetic and copies ran while one was open for 1% -> 0% of each run, Pallas kernels for 0% -> 0%
where the time goes in v1:
time: 38.5 us; the launch traced here: 38.3 us
  Pallas kernels  33.3 us (86%)
  local copies, waits for them, and re-layouts  4.25 us (11%)
  between operations  0.66 us (2%)
    pallas_call x1, Pallas kernels, shards(): pl.pallas_call(functools.partial(kernel, n_row, n_col, total_rows), out_s...  33.3 us
    unnamed x11, local copies, waits for them, and re-layouts  4.25 us

profile of v1, /device:TPU:0, one launch (start us, length us, event | category | flops | bytes accessed | tf_op | source)
XLA Modules:
  0.0 38.3 jit_solution(10536172918799377503)
XLA Ops:
  0.6 0.0 copy-start.2
  0.6 0.0 copy-start.3
  0.7 0.6 %copy-done.2 = s32[1,1,4]{2,1,0:T(1,128)S(1)} copy-done((s32[1,1,4]{2,1,0:T(1,128)S(1)}, s32[1,1,4]{2,1,0:T(1,128)}, u32[]{:S(2)}) %copy-start.2) | copy-done | bytes 40
  1.3 0.0 copy-done.3
  1.3 0.0 copy-start
  1.3 1.0 %copy-done = bf16[1,1,4,256,256]{4,3,2,1,0:T(8,128)(2,1)S(1)} copy-done((bf16[1,1,4,256,256]{4,3,2,1,0:T(8,128)(2,1)S(1)}, bf16[1,1,4,256,256]{4,3,2,1,0:T(8,128)(2,1)}, u32[]{:S(2)}) %copy-start) | copy-done | bytes 524312
  2.3 0.0 copy-start.1
  2.3 0.7 %copy-done.1 = bf16[32,256]{1,0:T(8,128)(2,1)S(1)} copy-done((bf16[32,256]{1,0:T(8,128)(2,1)S(1)}, bf16[32,256]{1,0:T(8,128)(2,1)}, u32[]{:S(2)}) %copy-start.1) | copy-done | bytes 16408
  3.1 33.3 %shard_map.67 = (f32[32,256]{1,0:T(8,128)S(1)}, f32[32,256]{1,0:T(8,128)S(1)}, f32[32,32]{1,0:T(8,128)S(1)}) custom-call(bf16[4,256,256]{2,1,0:T(8,128)(2,1)S(1)} %bitcast.3, s32[4]{0:T(128)S(1)} %bitcast.4, s32[4]{0:T(128)S(1)} %bitcast.5, bf16[32,256]{1,0:T(8,128)(2,1)S(1)} %copy-done.1), custom_call_target="tpu_custom_call" | custom-call | tf_op jit(solution)/shard_map/pallas_call | solution.py:222
  36.4 0.6 %copy.10 = f32[32,256]{1,0:T(8,128)} copy(f32[32,256]{1,0:T(8,128)S(1)} %get-tuple-element.6) | data formatting | bytes 65536
  37.0 0.6 %copy.11 = f32[32,256]{1,0:T(8,128)} copy(f32[32,256]{1,0:T(8,128)S(1)} %get-tuple-element.7) | data formatting | bytes 65536
  37.6 0.6 %copy.12 = f32[32,32]{1,0:T(8,128)} copy(f32[32,32]{1,0:T(8,128)S(1)} %get-tuple-element.8) | data formatting | bytes 8192
Async XLA Ops:
  0.6 0.7 %copy-start.2 = (s32[1,1,4]{2,1,0:T(1,128)S(1)}, s32[1,1,4]{2,1,0:T(1,128)}, u32[]{:S(2)}) copy-start(s32[1,1,4]{2,1,0:T(1,128)} %param.5) | copy-start | bytes 52
  0.6 0.7 %copy-start.3 = (s32[1,1,4]{2,1,0:T(1,128)S(1)}, s32[1,1,4]{2,1,0:T(1,128)}, u32[]{:S(2)}) copy-start(s32[1,1,4]{2,1,0:T(1,128)} %param.6) | copy-start | bytes 52
  1.3 1.0 %copy-start = (bf16[1,1,4,256,256]{4,3,2,1,0:T(8,128)(2,1)S(1)}, bf16[1,1,4,256,256]{4,3,2,1,0:T(8,128)(2,1)}, u32[]{:S(2)}) copy-start(bf16[1,1,4,256,256]{4,3,2,1,0:T(8,128)(2,1)} %param.4) | copy-start | bytes 1572868
  2.3 0.7 %copy-start.1 = (bf16[32,256]{1,0:T(8,128)(2,1)S(1)}, bf16[32,256]{1,0:T(8,128)(2,1)}, u32[]{:S(2)}) copy-start(bf16[32,256]{1,0:T(8,128)(2,1)} %x_ref.1) | copy-start | bytes 49156

commit v2 on v1

v2 whole, which is shorter than its diff:
```python
import functools

import jax
import jax.numpy as jnp
from jax import lax
from jax.experimental import pallas as pl
from jax.experimental.pallas import tpu as pltpu
from jax.sharding import PartitionSpec as P

VMEM_BYTES = 62 * 1024 * 1024
MESH = pl.DeviceIdType.MESH
F32 = jnp.float32
BF16 = jnp.bfloat16
NT = (((1,), (1,)), ((), ()))


def exact_dot(left, right):
    return jnp.dot(left, right, precision=lax.Precision.HIGHEST, preferred_element_type=F32)


def exact_dot_nt(left, right):
    return lax.dot_general(
        left, right, NT, precision=lax.Precision.HIGHEST, preferred_element_type=F32
    )


def offsets(size):
    return sorted(range(1, size), key=lambda d: -min(d, size - d))


def pack(square):
    k = square.shape[0]
    per = 128 // k
    rows = k // per
    return jnp.concatenate([square[i * rows : (i + 1) * rows] for i in range(per)], axis=1)


def unpack(packed, k):
    per = 128 // k
    return jnp.concatenate([packed[:, i * k : (i + 1) * k] for i in range(per)], axis=0)


def start_elimination(gram):
    k = gram.shape[0]
    eye = (
        lax.broadcasted_iota(jnp.int32, (k, k), 0) == lax.broadcasted_iota(jnp.int32, (k, k), 1)
    ).astype(F32)
    return jnp.concatenate([gram, eye], axis=1), jnp.zeros((k, 2 * k), F32)


def eliminate(work, out, first, last):
    k = work.shape[0]
    row_id = lax.broadcasted_iota(jnp.int32, (k, 2 * k), 0)
    for i in range(first, last):
        scale = lax.rsqrt(work[i : i + 1, i : i + 1])
        row = work[i : i + 1, :] * scale
        column = work[:, i : i + 1] * scale
        out = jnp.where(row_id == i, row, out)
        if i < k - 1:
            work = work - column * row
    return work, out


def kernel(
    n_row, n_col, total_rows,
    tiles_hbm, trow_hbm, tcol_hbm, x_hbm,
    ritz_hbm, res_hbm, proj_hbm,
    ritz_ref, res_ref, proj_ref, col_x0, col_x1, row_x0, row_x1, y_bf, dir_out, mir_out, dir_in, mir_in, small_row, small_col,
    tiles_ref, trow_ref, tcol_ref, send_sem, recv_sem, load_sem, store_sem,
):
    col_x, row_x = (col_x0, col_x1), (row_x0, row_x1)
    my_row = lax.axis_index("row")
    my_col = lax.axis_index("col")
    tile_count = tiles_ref.shape[0]
    k = x_hbm.shape[0]

    def row_peer(d):
        return (lax.rem(my_row + d, n_row), my_col)

    def col_peer(d):
        return (my_row, lax.rem(my_col + d, n_col))

    barrier = pltpu.get_barrier_semaphore()
    for d in range(1, n_row):
        pl.semaphore_signal(barrier, inc=1, device_id=row_peer(d), device_id_type=MESH)
    for d in range(1, n_col):
        pl.semaphore_signal(barrier, inc=1, device_id=col_peer(d), device_id_type=MESH)

    loads = [
        pltpu.make_async_copy(src, dst, load_sem.at[i])
        for i, (src, dst) in enumerate((
            (x_hbm, col_x[0].at[my_row]),
            (x_hbm, row_x[0].at[my_col]),
            (tcol_hbm, tcol_ref),
            (trow_hbm, trow_ref),
            (tiles_hbm, tiles_ref),
        ))
    ]
    for load in loads:
        load.start()
    stores = [
        pltpu.make_async_copy(src, dst, store_sem.at[i])
        for i, (src, dst) in enumerate(
            ((ritz_ref, ritz_hbm), (res_ref, res_hbm), (proj_ref, proj_hbm))
        )
    ]
    loads[0].wait()
    pl.semaphore_wait(barrier, n_row + n_col - 2)

    def send(src, dst, channel, peer):
        pltpu.make_async_remote_copy(
            src_ref=src, dst_ref=dst, send_sem=send_sem.at[channel], recv_sem=recv_sem.at[channel],
            device_id=peer, device_id_type=MESH,
        ).start()

    def wait_in(ref, channel):
        pltpu.make_async_copy(ref, ref, recv_sem.at[channel]).wait()

    def wait_out(ref, channel):
        pltpu.make_async_copy(ref, ref, send_sem.at[channel]).wait()

    def gather_start(src, p):
        for d in offsets(n_row):
            send(src, col_x[p].at[my_row], 4 * p, row_peer(d))
        for d in offsets(n_col):
            send(src, row_x[p].at[my_col], 4 * p + 1, col_peer(d))

    def gather_wait(p):
        wait_in(col_x[p].at[pl.ds(0, n_row - 1)], 4 * p)
        wait_in(row_x[p].at[pl.ds(0, n_col - 1)], 4 * p + 1)

    def small_start(p, which):
        if which == 0:
            for d in offsets(n_row):
                send(small_row.at[p, my_row], small_row.at[p, my_row], 8 + 2 * p, row_peer(d))
        else:
            for d in offsets(n_col):
                send(small_col.at[p, my_col], small_col.at[p, my_col], 9 + 2 * p, col_peer(d))

    def small_sum(p, which):
        ref, size = ((small_row, n_row), (small_col, n_col))[which]
        wait_in(ref.at[p, pl.ds(0, size - 1)], 8 + 2 * p + which)
        value = ref[p, 0]
        for i in range(1, size):
            value = value + ref[p, i]
        return value

    def bucket(parts, index_ref, slot):
        value = None
        for t in range(tile_count):
            term = jnp.where(index_ref[t] == slot, parts[t], 0.0)
            value = term if value is None else value + term
        return value.astype(BF16)

    def mirror_start(p):
        mirror = [
            jnp.dot(row_x[p][trow_ref[t]], tiles_ref[t], preferred_element_type=F32)
            for t in range(tile_count)
        ]
        for d in offsets(n_row):
            peer = row_peer(d)
            mir_out[p, d] = bucket(mirror, tcol_ref, peer[0])
            send(mir_out.at[p, d], mir_in.at[p, d - 1], 4 * p + 2, peer)
        mir_out[p, 0] = bucket(mirror, tcol_ref, my_row)

    def direct_start(p):
        direct = [
            lax.dot_general(col_x[p][tcol_ref[t]], tiles_ref[t], NT, preferred_element_type=F32)
            for t in range(tile_count)
        ]
        for d in offsets(n_col):
            peer = col_peer(d)
            dir_out[p, d] = bucket(direct, trow_ref, peer[1])
            send(dir_out.at[p, d], dir_in.at[p, d - 1], 4 * p + 3, peer)
        dir_out[p, 0] = bucket(direct, trow_ref, my_col)
        return direct

    def scatter_sum(p):
        value = dir_out[p, 0].astype(F32) + mir_out[p, 0].astype(F32)
        wait_in(dir_in.at[p], 4 * p + 3)
        for i in range(n_col - 1):
            value = value + dir_in[p, i].astype(F32)
        wait_in(mir_in.at[p], 4 * p + 2)
        for i in range(n_row - 1):
            value = value + mir_in[p, i].astype(F32)
        return value

    gather_start(col_x[0].at[my_row], 0)
    for load in loads[1:]:
        load.wait()
    gather_wait(0)
    mirror_start(0)
    direct_start(0)
    image = scatter_sum(0)

    y_bf[...] = image.astype(BF16)
    gather_start(y_bf, 1)
    col_x[1][my_row] = y_bf[...]
    row_x[1][my_col] = y_bf[...]
    small_col[0, my_col] = pack(exact_dot_nt(image, image))
    small_start(0, 1)
    small_row[0, my_row] = small_sum(0, 1)
    small_start(0, 0)
    gather_wait(1)
    mirror_start(1)
    direct = direct_start(1)
    cross = None
    for t in range(tile_count):
        row_pick = row_x[1][trow_ref[t]]
        high = direct[t].astype(BF16)
        low = (direct[t] - high.astype(F32)).astype(BF16)
        for part in (high, low):
            term = lax.dot_general(row_pick, part, NT, preferred_element_type=F32)
            cross = term if cross is None else cross + term
    small_col[1, my_col] = pack(cross)
    small_start(1, 1)
    work, out = start_elimination(unpack(small_sum(0, 0), k) / total_rows)
    work, out = eliminate(work, out, 0, k // 2)
    small_row[1, my_row] = small_sum(1, 1)
    small_start(1, 0)
    work, out = eliminate(work, out, k // 2, k)
    inverse = out[:, k:]
    ritz = exact_dot(inverse, image)
    ritz_ref[...] = ritz
    stores[0].start()
    half = unpack(small_sum(1, 0), k) / total_rows
    half = exact_dot_nt(exact_dot(inverse, half), inverse)
    projected = half + half.T
    proj_ref[...] = projected
    stores[2].start()
    expected = exact_dot(projected, ritz)
    last = scatter_sum(1)
    res_ref[...] = exact_dot(inverse, last) - expected
    stores[1].start()

    for p in range(2):
        wait_out(col_x[p].at[pl.ds(0, n_row - 1)], 4 * p)
        wait_out(row_x[p].at[pl.ds(0, n_col - 1)], 4 * p + 1)
        wait_out(mir_in.at[p], 4 * p + 2)
        wait_out(dir_in.at[p], 4 * p + 3)
        wait_out(small_row.at[p, pl.ds(0, n_row - 1)], 8 + 2 * p)
        wait_out(small_col.at[p, pl.ds(0, n_col - 1)], 9 + 2 * p)
    for store in stores:
        store.wait()


def write_out(*refs):
    count = (len(refs) - 1) // 2
    sems = refs[-1]
    copies = [
        pltpu.make_async_copy(refs[i], refs[count + i], sems.at[i]) for i in range(count)
    ]
    for copy in copies:
        copy.start()
    for copy in copies:
        copy.wait()


def shards(n_row, n_col, tile_values, tile_row, tile_col, basis_init):
    k, m = basis_init.shape
    tiles = tile_values[0, 0]
    total_rows = m * n_row * n_col
    packed = (k * k // 128, 128)
    hbm = pl.BlockSpec(memory_space=pltpu.HBM)
    out_shape = (
        jax.ShapeDtypeStruct((k, m), F32),
        jax.ShapeDtypeStruct((k, m), F32),
        jax.ShapeDtypeStruct((k, k), F32),
    )
    results = pl.pallas_call(
        functools.partial(kernel, n_row, n_col, total_rows),
        out_shape=out_shape,
        in_specs=[hbm] * 4,
        out_specs=(hbm,) * 3,
        scratch_shapes=[pltpu.VMEM(shape.shape, F32) for shape in out_shape]
        + [
            pltpu.VMEM((n_row, k, m), BF16),
            pltpu.VMEM((n_row, k, m), BF16),
            pltpu.VMEM((n_col, k, m), BF16),
            pltpu.VMEM((n_col, k, m), BF16),
            pltpu.VMEM((k, m), BF16),
            pltpu.VMEM((2, n_col, k, m), BF16),
            pltpu.VMEM((2, n_row, k, m), BF16),
            pltpu.VMEM((2, n_col - 1, k, m), BF16),
            pltpu.VMEM((2, n_row - 1, k, m), BF16),
            pltpu.VMEM((2, n_row) + packed, F32),
            pltpu.VMEM((2, n_col) + packed, F32),
            pltpu.VMEM(tiles.shape, BF16),
            pltpu.SMEM((tiles.shape[0],), jnp.int32),
            pltpu.SMEM((tiles.shape[0],), jnp.int32),
            pltpu.SemaphoreType.DMA((12,)),
            pltpu.SemaphoreType.DMA((12,)),
            pltpu.SemaphoreType.DMA((5,)),
            pltpu.SemaphoreType.DMA((3,)),
        ],
        compiler_params=pltpu.CompilerParams(
            collective_id=0, has_side_effects=True, vmem_limit_bytes=VMEM_BYTES
        ),
    )(tiles, tile_row[0, 0], tile_col[0, 0], basis_init)
    return pl.pallas_call(
        write_out,
        out_shape=out_shape,
        in_specs=[hbm] * 3,
        out_specs=(hbm,) * 3,
        scratch_shapes=[pltpu.SemaphoreType.DMA((3,))],
    )(*results)


def solution(mesh):
    return jax.shard_map(
        functools.partial(shards, mesh.shape["row"], mesh.shape["col"]),
        mesh=mesh,
        in_specs=(
            P("row", "col", None, None, None),
            P("row", "col", None),
            P("row", "col", None),
            P(None, ("col", "row")),
        ),
        out_specs=(P(None, ("col", "row")), P(None, ("col", "row")), P()),
        check_vma=False,
    )
```

time: 38.5 us -> 37.2 us (0.966)
  local copies, waits for them, and re-layouts: 4.25 us -> 0 us
  Pallas kernels: 33.3 us -> 36.3 us
    unnamed x11 -> x0, local copies, waits for them, and re-layouts: 4.25 us -> none
    pallas_call x0 -> x1, Pallas kernels: none -> 3.61 us  [shards(): pl.pallas_call(write_out, out_shape=out_shape, in_specs=[hbm] * 3, out_sp...]
    pallas_call x1, Pallas kernels: 33.3 us -> 32.7 us  [shards(): pl.pallas_call(functools.partial(kernel, n_row, n_col, total_rows), out_s...]
where the time goes in v2:
time: 37.2 us; the launch traced here: 36.9 us
  Pallas kernels  36.3 us (98%)
  between operations  0.64 us (2%)
    pallas_call x1, Pallas kernels, shards(): pl.pallas_call(functools.partial(kernel, n_row, n_col, total_rows), out_s...  32.7 us
    pallas_call x1, Pallas kernels, shards(): pl.pallas_call(write_out, out_shape=out_shape, in_specs=[hbm] * 3, out_sp...  3.61 us

profile of v2, /device:TPU:0, one launch (start us, length us, event | category | flops | bytes accessed | tf_op | source)
XLA Modules:
  0.0 36.9 jit_solution(11385926587897581538)
XLA Ops:
  0.6 32.7 %shard_map.67 = (f32[32,256]{1,0:T(8,128)}, f32[32,256]{1,0:T(8,128)}, f32[32,32]{1,0:T(8,128)}) custom-call(bf16[4,256,256]{2,1,0:T(8,128)(2,1)} %bitcast.3, s32[4]{0:T(128)} %bitcast.4, s32[4]{0:T(128)} %bitcast.5, bf16[32,256]{1,0:T(8,128)(2,1)} %x_hbm.1), custom_call_target="tpu_custom_call" | custom-call | tf_op jit(solution)/shard_map/pallas_call | solution.py:270
  33.3 3.6 %shard_map.68 = (f32[32,256]{1,0:T(8,128)}, f32[32,256]{1,0:T(8,128)}, f32[32,32]{1,0:T(8,128)}) custom-call(f32[32,256]{1,0:T(8,128)} %get-tuple-element.6.refs_0_, f32[32,256]{1,0:T(8,128)} %get-tuple-element.7.refs_1_, f32[32,32]{1,0:T(8,128)} %get-tuple-element.8.refs_2_), custom_call_target="tpu_custom_call" | custom-call | tf_op jit(solution)/shard_map/pallas_call | solution.py:300

commit v3 on v2

--- a/solution.py
+++ b/solution.py
@@ -163,17 +163,18 @@
             send(mir_out.at[p, d], mir_in.at[p, d - 1], 4 * p + 2, peer)
         mir_out[p, 0] = bucket(mirror, tcol_ref, my_row)
 
-    def direct_start(p):
-        direct = [
+    def direct_products(p):
+        return [
             lax.dot_general(col_x[p][tcol_ref[t]], tiles_ref[t], NT, preferred_element_type=F32)
             for t in range(tile_count)
         ]
+
+    def direct_start(p, direct):
         for d in offsets(n_col):
             peer = col_peer(d)
             dir_out[p, d] = bucket(direct, trow_ref, peer[1])
             send(dir_out.at[p, d], dir_in.at[p, d - 1], 4 * p + 3, peer)
         dir_out[p, 0] = bucket(direct, trow_ref, my_col)
-        return direct
 
     def scatter_sum(p):
         value = dir_out[p, 0].astype(F32) + mir_out[p, 0].astype(F32)
@@ -190,7 +191,7 @@
         load.wait()
     gather_wait(0)
     mirror_start(0)
-    direct_start(0)
+    direct_start(0, direct_products(0))
     image = scatter_sum(0)
 
     y_bf[...] = image.astype(BF16)
@@ -202,8 +203,7 @@
     small_row[0, my_row] = small_sum(0, 1)
     small_start(0, 0)
     gather_wait(1)
-    mirror_start(1)
-    direct = direct_start(1)
+    direct = direct_products(1)
     cross = None
     for t in range(tile_count):
         row_pick = row_x[1][trow_ref[t]]
@@ -214,11 +214,13 @@
             cross = term if cross is None else cross + term
     small_col[1, my_col] = pack(cross)
     small_start(1, 1)
+    mirror_start(1)
+    direct_start(1, direct)
     work, out = start_elimination(unpack(small_sum(0, 0), k) / total_rows)
-    work, out = eliminate(work, out, 0, k // 2)
+    work, out = eliminate(work, out, 0, k // 4)
     small_row[1, my_row] = small_sum(1, 1)
     small_start(1, 0)
-    work, out = eliminate(work, out, k // 2, k)
+    work, out = eliminate(work, out, k // 4, k)
     inverse = out[:, k:]
     ritz = exact_dot(inverse, image)
     ritz_ref[...] = ritz
@@ -245,15 +247,21 @@
 
 
 def write_out(*refs):
-    count = (len(refs) - 1) // 2
-    sems = refs[-1]
-    copies = [
-        pltpu.make_async_copy(refs[i], refs[count + i], sems.at[i]) for i in range(count)
+    results, outputs, staged = refs[:3], refs[3:6], refs[6:9]
+    load_sem, store_sem = refs[9:]
+    loads = [
+        pltpu.make_async_copy(results[i], staged[i], load_sem.at[i]) for i in range(3)
     ]
-    for copy in copies:
-        copy.start()
-    for copy in copies:
-        copy.wait()
+    stores = [
+        pltpu.make_async_copy(staged[i], outputs[i], store_sem.at[i]) for i in range(3)
+    ]
+    for load in loads:
+        load.start()
+    for load, store in zip(loads, stores):
+        load.wait()
+        store.start()
+    for store in stores:
+        store.wait()
 
 
 def shards(n_row, n_col, tile_values, tile_row, tile_col, basis_init):
@@ -302,7 +310,8 @@
         out_shape=out_shape,
         in_specs=[hbm] * 3,
         out_specs=(hbm,) * 3,
-        scratch_shapes=[pltpu.SemaphoreType.DMA((3,))],
+        scratch_shapes=[pltpu.VMEM(shape.shape, F32) for shape in out_shape]
+        + [pltpu.SemaphoreType.DMA((3,)), pltpu.SemaphoreType.DMA((3,))],
     )(*results)
 
 

time: 37.2 us -> 35.1 us (0.944)
  Pallas kernels: 36.3 us -> 34.2 us
    pallas_call x1, Pallas kernels: 3.61 us -> 1.44 us  [shards(): pl.pallas_call(write_out, out_shape=out_shape, in_specs=[hbm] * 3, out_sp...]
where the time goes in v3:
time: 35.1 us; the launch traced here: 34.9 us
  Pallas kernels  34.2 us (97%)
  between operations  0.64 us (2%)
    pallas_call x1, Pallas kernels, shards(): pl.pallas_call(functools.partial(kernel, n_row, n_col, total_rows), out_s...  32.8 us
    pallas_call x1, Pallas kernels, shards(): pl.pallas_call(write_out, out_shape=out_shape, in_specs=[hbm] * 3, out_sp...  1.44 us

profile of v3, /device:TPU:0, one launch (start us, length us, event | category | flops | bytes accessed | tf_op | source)
XLA Modules:
  0.0 34.9 jit_solution(17512600961893994531)
XLA Ops:
  0.6 32.8 %shard_map.67 = (f32[32,256]{1,0:T(8,128)}, f32[32,256]{1,0:T(8,128)}, f32[32,32]{1,0:T(8,128)}) custom-call(bf16[4,256,256]{2,1,0:T(8,128)(2,1)} %bitcast.3, s32[4]{0:T(128)} %bitcast.4, s32[4]{0:T(128)} %bitcast.5, bf16[32,256]{1,0:T(8,128)(2,1)} %x_hbm.1), custom_call_target="tpu_custom_call" | custom-call | tf_op jit(solution)/shard_map/pallas_call | solution.py:278
  33.4 1.4 %shard_map.68 = (f32[32,256]{1,0:T(8,128)}, f32[32,256]{1,0:T(8,128)}, f32[32,32]{1,0:T(8,128)}) custom-call(f32[32,256]{1,0:T(8,128)} %get-tuple-element.6.refs_0_, f32[32,256]{1,0:T(8,128)} %get-tuple-element.7.refs_1_, f32[32,32]{1,0:T(8,128)} %get-tuple-element.8.refs_2_), custom_call_target="tpu_custom_call" | custom-call | tf_op jit(solution)/shard_map/pallas_call | solution.py:308

commit v4 on v3

--- a/solution.py
+++ b/solution.py
@@ -214,13 +214,13 @@
             cross = term if cross is None else cross + term
     small_col[1, my_col] = pack(cross)
     small_start(1, 1)
+    work, out = start_elimination(unpack(small_sum(0, 0), k) / total_rows)
+    work, out = eliminate(work, out, 0, k // 2)
+    small_row[1, my_row] = small_sum(1, 1)
+    small_start(1, 0)
     mirror_start(1)
     direct_start(1, direct)
-    work, out = start_elimination(unpack(small_sum(0, 0), k) / total_rows)
-    work, out = eliminate(work, out, 0, k // 4)
-    small_row[1, my_row] = small_sum(1, 1)
-    small_start(1, 0)
-    work, out = eliminate(work, out, k // 4, k)
+    work, out = eliminate(work, out, k // 2, k)
     inverse = out[:, k:]
     ritz = exact_dot(inverse, image)
     ritz_ref[...] = ritz

time: 35.1 us -> 35.2 us (level)
  no operation moved by 1% of the time
where the time goes in v4:
time: 35.2 us; the launch traced here: 34.9 us
  Pallas kernels  34.3 us (97%)
  between operations  0.64 us (2%)
    pallas_call x1, Pallas kernels, shards(): pl.pallas_call(functools.partial(kernel, n_row, n_col, total_rows), out_s...  32.8 us
    pallas_call x1, Pallas kernels, shards(): pl.pallas_call(write_out, out_shape=out_shape, in_specs=[hbm] * 3, out_sp...  1.44 us

profile of v4, /device:TPU:0, one launch (start us, length us, event | category | flops | bytes accessed | tf_op | source)
XLA Modules:
  0.0 34.9 jit_solution(2497320609768214958)
XLA Ops:
  0.6 32.8 %shard_map.67 = (f32[32,256]{1,0:T(8,128)}, f32[32,256]{1,0:T(8,128)}, f32[32,32]{1,0:T(8,128)}) custom-call(bf16[4,256,256]{2,1,0:T(8,128)(2,1)} %bitcast.3, s32[4]{0:T(128)} %bitcast.4, s32[4]{0:T(128)} %bitcast.5, bf16[32,256]{1,0:T(8,128)(2,1)} %x_hbm.1), custom_call_target="tpu_custom_call" | custom-call | tf_op jit(solution)/shard_map/pallas_call | solution.py:278
  33.5 1.4 %shard_map.68 = (f32[32,256]{1,0:T(8,128)}, f32[32,256]{1,0:T(8,128)}, f32[32,32]{1,0:T(8,128)}) custom-call(f32[32,256]{1,0:T(8,128)} %get-tuple-element.6.refs_0_, f32[32,256]{1,0:T(8,128)} %get-tuple-element.7.refs_1_, f32[32,32]{1,0:T(8,128)} %get-tuple-element.8.refs_2_), custom_call_target="tpu_custom_call" | custom-call | tf_op jit(solution)/shard_map/pallas_call | solution.py:308

commit v5 on v3

--- a/solution.py
+++ b/solution.py
@@ -25,7 +25,7 @@
 
 
 def offsets(size):
-    return sorted(range(1, size), key=lambda d: -min(d, size - d))
+    return sorted(range(1, size), key=lambda d: min(d, size - d))
 
 
 def pack(square):

time: 35.1 us -> 33.5 us (0.954)
  Pallas kernels: 34.2 us -> 32.7 us
    pallas_call x1, Pallas kernels: 32.8 us -> 31.2 us  [shards(): pl.pallas_call(functools.partial(kernel, n_row, n_col, total_rows), out_s...]
where the time goes in v5:
time: 33.5 us; the launch traced here: 33.3 us
  Pallas kernels  32.7 us (98%)
  between operations  0.64 us (2%)
    pallas_call x1, Pallas kernels, shards(): pl.pallas_call(functools.partial(kernel, n_row, n_col, total_rows), out_s...  31.2 us
    pallas_call x1, Pallas kernels, shards(): pl.pallas_call(write_out, out_shape=out_shape, in_specs=[hbm] * 3, out_sp...  1.44 us

profile of v5, /device:TPU:0, one launch (start us, length us, event | category | flops | bytes accessed | tf_op | source)
XLA Modules:
  0.0 33.3 jit_solution(17158838629898035099)
XLA Ops:
  0.6 31.2 %shard_map.67 = (f32[32,256]{1,0:T(8,128)}, f32[32,256]{1,0:T(8,128)}, f32[32,32]{1,0:T(8,128)}) custom-call(bf16[4,256,256]{2,1,0:T(8,128)(2,1)} %bitcast.3, s32[4]{0:T(128)} %bitcast.4, s32[4]{0:T(128)} %bitcast.5, bf16[32,256]{1,0:T(8,128)(2,1)} %x_hbm.1), custom_call_target="tpu_custom_call" | custom-call | tf_op jit(solution)/shard_map/pallas_call | solution.py:278
  31.8 1.4 %shard_map.68 = (f32[32,256]{1,0:T(8,128)}, f32[32,256]{1,0:T(8,128)}, f32[32,32]{1,0:T(8,128)}) custom-call(f32[32,256]{1,0:T(8,128)} %get-tuple-element.6.refs_0_, f32[32,256]{1,0:T(8,128)} %get-tuple-element.7.refs_1_, f32[32,32]{1,0:T(8,128)} %get-tuple-element.8.refs_2_), custom_call_target="tpu_custom_call" | custom-call | tf_op jit(solution)/shard_map/pallas_call | solution.py:308
